TPU v7x, 1024 devices: a whole 8x8x8 slice. The times are simulated.
1024 devices in a mesh: gx: 16 (over z, core), gy: 64 (over y, x).
Axes of the slice: x: 8, y: 8, z: 8, core: 2. Of those that a mesh axis runs over, the one named last changes fastest.
Arguments:
- start_field: float32 [64, 32, 256, 128], P(None, 'gx', 'gy'), may hold values from -6 to 6
- right_side: float32 [64, 32, 256, 128], P(None, 'gx', 'gy'), may hold values from -6 to 6
- coefficient: float32 [32, 256, 128], P('gx', 'gy'), may hold values from 1 to 10
- stiffness: float32 [64, 64], replicated, may hold values from -0.6 to 4.6, as said below
- smoother: float32 [64, 64], replicated, may hold values from -0.03 to 0.23, as said below
- face_coupling: float32 [6, 64, 64], replicated, may hold values from -0.12 to 0.12
- prolongation: float32 [2, 2, 2, 64, 64], replicated, may hold values from -0.75 to 0.75
Outputs:
- solution_field: float32 [64, 32, 256, 128], P(None, 'gx', 'gy')
Inputs may be any that keep to these rules, and one draw needn't show every extreme that they name: `stiffness`: diagonal entries lie in 3.4 to 4.6, the others in -0.6 to 0.6. `smoother`: diagonal entries lie in 0.17 to 0.23, the others in -0.03 to 0.03.
All inputs are finite; a program needn't handle non-finite values.
Results may differ from a plain program's by a relative error of at most 0.00015.
Values sent between devices are 32-bit elements; how exact they have to be, the bound alone decides.
A program may use at most 32 MiB of HBM per device.

v0:
```python
import jax
import jax.numpy as jnp
from jax import lax
from jax.experimental import pallas as pl
from jax.experimental.pallas import tpu as pltpu
from jax.sharding import PartitionSpec as P

MESH = pl.DeviceIdType.MESH
F32 = jnp.float32
BF16 = jnp.bfloat16
D = 64
L = 128
XLO, CEN, ZLO, ZHI, YLO, YHI, XHI = range(7)


def parts(x):
    hi = x.astype(BF16)
    lo = (x - hi.astype(F32)).astype(BF16)
    return hi, lo


def split_rows(x):
    hi, lo = parts(x)
    return jnp.concatenate([hi, hi, lo, lo], axis=0)


def dot(a, b):
    return jnp.dot(a, b, preferred_element_type=F32)


def roll(x, shift, axis=1):
    return pltpu.roll(x, shift % x.shape[axis], axis)


def col(c):
    return slice(c * L, (c + 1) * L)


def kernel(nx, ny, v_in, b_in, k_in, s_in, m_in, f_in, p_in, out,
           v_raw, b_raw, k_raw, s_raw, m_raw, f_raw, p_raw,
           v0, v1, v2, v3, rhs, const, res, lifted, part0, part1, part2, part3, prod, prod1,
           hx0, hy0, hx1, hy1, hpx1, hpy1, hx2, hy2, hpx3, hpy3, hx3, hy3, edge1, edge3, corner2, corner_c2, hk, hkc, c1, c2, hc1, hc2,
           gst, rst, pst, qst, gpx, gpy, ghx, ghy, alpha, calpha, krow, local_sem, send_sem, recv_sem):
    gx, gy = lax.axis_index("gx"), lax.axis_index("gy")
    has = {(-1, 0): gx > 0, (1, 0): gx < nx - 1, (0, -1): gy > 0, (0, 1): gy < ny - 1}
    for dx in (-1, 1):
        for dy in (-1, 1):
            has[dx, dy] = jnp.logical_and(has[dx, 0], has[0, dy])
    faces = ((0, -1), (0, 1), (-1, 0), (1, 0))
    diagonals = ((-1, -1), (-1, 1), (1, -1), (1, 1))
    odd = lax.rem(gx, 2)
    away_x = gx + 2 * odd - 1
    has_away = jnp.logical_and(away_x >= 0, away_x < nx)

    loads = [pltpu.make_async_copy(src, dst, local_sem.at[i]) for i, (src, dst) in enumerate(
        ((k_in, k_raw), (v_in, v_raw), (m_in, m_raw), (s_in, s_raw), (f_in, f_raw), (b_in, b_raw), (p_in, p_raw)))]
    barrier = pltpu.get_barrier_semaphore()
    for d in faces:
        @pl.when(has[d])
        def _(d=d):
            pl.semaphore_signal(barrier, inc=1, device_id=(gx + d[0], gy + d[1]), device_id_type=MESH)
    for load in loads[:2]:
        load.start()

    sent = []

    def put(src, dst, device, out_if, in_if):
        slot = len(sent)
        copy = pltpu.make_async_remote_copy(
            src_ref=src, dst_ref=dst, send_sem=send_sem.at[slot], recv_sem=recv_sem.at[slot],
            device_id=device, device_id_type=MESH)
        pl.when(out_if)(copy.start)
        sent.append((copy, out_if))
        return copy, in_if

    def send(src, dst, d):
        return put(src, dst, (gx + d[0], gy + d[1]), has[d], has[-d[0], -d[1]])

    def relay(src, dst, j):
        there = has[0, 2 * j - 1]
        return put(src, dst, (gx + 1 - 2 * odd, gy), there, there)

    def arrive(*copies):
        for copy, in_if in copies:
            pl.when(in_if)(copy.wait_recv)

    def send_y(v, hy):
        return [send(v.at[:, :, col(3)], hy.at[0], (0, 1)), send(v.at[:, :, col(0)], hy.at[1], (0, -1))]

    def send_x(v, hx):
        return [send(v.at[1], hx.at[0], (1, 0)), send(v.at[0], hx.at[1], (-1, 0))]

    def send_edges(v, edge):
        return [put(v.at[odd, :, col(3 if dy > 0 else 0)], edge.at[2 * (1 - odd) + (1 - dy) // 2], (away_x, gy + dy),
                    jnp.logical_and(has_away, has[0, dy]), jnp.logical_and(has_away, has[0, -dy])) for dy in (-1, 1)]

    def send_tile(c, h):
        return (send(c, h.at[0], (0, 1)), send(c, h.at[1], (0, -1)), send(c, h.at[2], (1, 0)), send(c, h.at[3], (-1, 0)))

    loads[1].wait()
    for load in loads[2:]:
        load.start()
    for c in range(8):
        v0[c // 4, :, col(c % 4)] = v_raw[pl.ds(c, D, stride=8), :]
    loads[0].wait()
    count = has[-1, 0].astype(jnp.int32) + has[1, 0].astype(jnp.int32) + has[0, -1].astype(jnp.int32) + has[0, 1].astype(jnp.int32)
    pl.semaphore_wait(barrier, count)
    kcopies = send_tile(k_raw, hk)
    first = send_y(v0, hy0) + send_x(v0, hx0)

    for d, y_at, x_at in (((0, -1), 0, None), ((0, 1), 1, None), ((-1, 0), None, 0), ((1, 0), None, 1)):
        @pl.when(jnp.logical_not(has[d]))
        def _(y_at=y_at, x_at=x_at):
            if x_at is None:
                for ref in (hy0, hy1, hpy1, hpy3):
                    ref[y_at] = jnp.zeros_like(ref[y_at])
                for ref in (hk, hc1, hc2):
                    ref[y_at] = jnp.zeros_like(ref[y_at])
                for i in range(2):
                    for ref in (edge1, edge3, corner2, corner_c2, hkc):
                        ref[2 * i + y_at] = jnp.zeros_like(ref[0])
            else:
                for ref in (hx0, hx1, hpx1, hpx3):
                    ref[x_at] = jnp.zeros_like(ref[x_at])
                for ref in (hk, hc1, hc2):
                    ref[2 + x_at] = jnp.zeros_like(ref[0])
                for j in range(2):
                    for ref in (edge1, edge3, corner2, corner_c2, hkc):
                        ref[2 * x_at + j] = jnp.zeros_like(ref[0])

    lane = lax.broadcasted_iota(jnp.int32, (D, L), 1)
    low_half = lane < D
    even = lax.rem(lane, 2) == 0
    row_even = even[:1]

    def twice(w):
        return jnp.concatenate([w, w], axis=1)

    def put_left(ref, rows, w, lanes=0):
        hi, lo = parts(w)
        both = jnp.where(low_half, hi.astype(F32), lo.astype(F32)).astype(BF16)
        ref[rows, lanes:lanes + L] = both
        ref[rows, lanes + L:lanes + 2 * L] = both

    def block(i):
        return slice(i * D, (i + 1) * D)

    for i in (2, 3, 4):
        loads[i].wait()
    m_hi, m_lo = parts(twice(m_raw[...]))
    m_both = jnp.where(low_half, m_hi.astype(F32), m_lo.astype(F32)).astype(BF16)
    m_left = jnp.concatenate([m_both, m_both], axis=1)
    order = ((XLO, 0), (XHI, 1), (YLO, 2), (YHI, 3), (ZLO, 4), (ZHI, 5))
    raw = {CEN: twice(s_raw[...])}
    for blk, face in order:
        raw[blk] = twice(f_raw[face])
    stacked = jnp.concatenate([raw[blk] for blk in range(7)], axis=1)
    folded = dot(m_left, split_rows(stacked))
    eye = (lax.rem(lane, D) == lax.broadcasted_iota(jnp.int32, (D, L), 0)).astype(F32)
    for blk in range(7):
        w = folded[:, col(blk)]
        put_left(gst, block(blk), eye - w if blk == CEN else w)

    loads[5].wait()
    k8 = k_raw[...]
    inv8 = 1.0 / k8
    for c in range(8):
        krow[c // 4, 0:1, col(c % 4)] = k8[c:c + 1]
        krow[c // 4, 1:2, col(c % 4)] = inv8[c:c + 1]
        rhs[c // 4, :, col(c % 4)] = b_raw[pl.ds(c, D, stride=8), :]
    for x in range(2):
        const[x] = dot(m_left, split_rows(rhs[x])) * krow[x, 1:2, :]

    def weigh(ke, kn):
        return jnp.where(kn > 0, 2.0 * kn / (ke + kn), 0.0)

    def weight(blk, c):
        return alpha[blk, c:c + 1, :]

    for blk in range(7):
        put_left(rst, block(blk), -raw[blk] if blk == CEN else raw[blk])
    loads[6].wait()
    twins, doubled = [], []
    for abc in range(8):
        w = twice(p_raw[abc])
        doubled.append(w)
        put_left(pst, block(abc), w)
        hi, lo = parts(w)
        right_form = jnp.concatenate([hi, lo], axis=1)
        twins += [right_form, right_form]
    for ref, i, blk, chosen in ((gpx, 0, XLO, (4, 5, 6, 7)), (gpx, 1, XHI, (0, 1, 2, 3)),
                                (gpy, 0, YLO, (2, 3, 6, 7)), (gpy, 1, YHI, (0, 1, 4, 5))):
        both = dot(gst[block(blk), :], split_rows(jnp.concatenate([doubled[abc] for abc in chosen], axis=1)))
        for n in range(4):
            put_left(ref.at[i], block(n), both[:, col(n)])
    folded_p = lax.dot_general(m_left, jnp.concatenate(twins, axis=0), (((1,), (1,)), ((), ())),
                               preferred_element_type=F32)
    for abc in range(8):
        ab, c = divmod(abc, 2)
        put_left(qst, block(c), folded_p[:, col(abc)], 2 * L * ab)

    row8 = lax.broadcasted_iota(jnp.int32, (8, L), 0)
    lane8 = lax.broadcasted_iota(jnp.int32, (8, L), 1)
    y8 = lax.rem(row8, 4)
    own_neighbours = {
        XLO: roll(k8, 4, 0),
        XHI: roll(k8, 4, 0),
        YLO: roll(k8, 1, 0),
        YHI: roll(k8, -1, 0),
        ZLO: jnp.where(lane8 == 0, 0.0, roll(k8, 1)),
        ZHI: jnp.where(lane8 == L - 1, 0.0, roll(k8, -1)),
    }
    for blk, kn in own_neighbours.items():
        alpha[blk] = weigh(k8, kn)

    ends_first = (0, 4, 3, 7, 1, 5, 2, 6)

    def own_part(target, v, stack, base, scale, prod, wide, ends_done=None):
        for x in range(2):
            rows = slice(0, 7 * D) if wide else slice(x * D, (6 + x) * D)
            prod[x, rows, :] = dot(stack[rows, :], split_rows(v[x]))
        for c in ends_first:
            x, y = divmod(c, 4)

            def term(blk, x, y):
                return prod[x, block(blk), col(y)]

            acc = term(CEN, x, y)
            acc += weight(ZLO, c) * roll(term(ZLO, x, y), 1)
            acc += weight(ZHI, c) * roll(term(ZHI, x, y), -1)
            if x == 0:
                acc += weight(XHI, c) * term(XHI, 1, y)
            else:
                acc += weight(XLO, c) * term(XLO, 0, y)
            if y > 0:
                acc += weight(YLO, c) * term(YLO, x, y - 1)
            if y < 3:
                acc += weight(YHI, c) * term(YHI, x, y + 1)
            if scale is not None:
                acc = acc * scale[x, 0:1, col(y)]
            target[x, :, col(y)] = base[x, :, col(y)] + acc
            if c == 7 and ends_done is not None:
                ends_done()

    def halo_products(stack, hx, hy, copies=(), passed_on=None):
        found_x, found_y = [], []
        arrive(*copies[:2])
        for j in range(2):
            if passed_on is not None:
                passed_on(j)
        arrive(*copies[2:])
        for j in range(2):
            found_y.append(dot(stack[block((YLO, YHI)[j]), :],
                               split_rows(jnp.concatenate([hy[j, 0], hy[j, 1]], axis=1))))
        for i in range(2):
            found_x.append(dot(stack[block((XLO, XHI)[i]), :], split_rows(hx[i])))
        return found_x + found_y

    def halo_part(target, part, products, scale, ends_done=None):
        from_xlo, from_xhi, from_ylo, from_yhi = products
        for c in ends_first:
            x, y = divmod(c, 4)
            acc = weight(XLO, c) * from_xlo[:, col(y)] if x == 0 else weight(XHI, c) * from_xhi[:, col(y)]
            if y == 0:
                acc += weight(YLO, c) * from_ylo[:, col(x)]
            if y == 3:
                acc += weight(YHI, c) * from_yhi[:, col(x)]
            if scale is not None:
                acc = acc * scale[x, 0:1, col(y)]
            value = part[x, :, col(y)] + acc
            if target is out:
                out[pl.ds(c, D, stride=8), :] = value
            else:
                target[x, :, col(y)] = value
            if c == 7 and ends_done is not None:
                ends_done()

    def complete_halo(hx, hy, hpx, hpy, edge, copies):
        arrive(*copies)

        def edges(i, j):
            return split_rows(jnp.concatenate([edge[i], edge[j]], axis=1))

        from_edge = {XLO: dot(gst[block(XLO), :], edges(0, 1)), XHI: dot(gst[block(XHI), :], edges(2, 3)),
                     YLO: dot(gst[block(YLO), :], edges(0, 2)), YHI: dot(gst[block(YHI), :], edges(1, 3))}
        kx, ky = (kxlo, kxhi), (kylo, kyhi)
        for i in range(2):
            mine, theirs = ((XLO, XHI), (XHI, XLO))[i]
            for y in range(4):
                c = 4 * i + y
                value = hpx[i, :, col(y)] + (2.0 - weight(mine, c)) * prod1[i, block(theirs), col(y)]
                if y in (0, 3):
                    j = y // 3
                    w = weigh(kx[i][4 * (1 - i) + y:4 * (1 - i) + y + 1],
                              hkc[2 * i + j][4 * (1 - i) + 3 - y:4 * (1 - i) + 4 - y])
                    value += w * from_edge[(YLO, YHI)[j]][:, col(i)]
                hx[i, :, col(y)] = value
        for j in range(2):
            mine, theirs = ((YLO, YHI), (YHI, YLO))[j]
            y = 3 * j
            for x in range(2):
                value = hpy[j, x] + (2.0 - weight(mine, 4 * x + y)) * prod1[x, block(theirs), col(y)]
                e, n = 4 * x + 3 - y, 4 * (1 - x) + 3 - y
                w = weigh(ky[j][e:e + 1], hkc[2 * x + j][n:n + 1])
                value += w * from_edge[(XLO, XHI)[x]][:, col(j)]
                hy[j, x] = value

    later = []
    own_part(part0, v0, gst, const, None, prod, False)
    arrive(*kcopies)
    kylo, kyhi, kxlo, kxhi = (hk[i] for i in range(4))
    neighbours = {
        XLO: jnp.where(row8 < 4, roll(kxlo, 4, 0), own_neighbours[XLO]),
        XHI: jnp.where(row8 < 4, own_neighbours[XHI], roll(kxhi, 4, 0)),
        YLO: jnp.where(y8 == 0, roll(kylo, -3, 0), own_neighbours[YLO]),
        YHI: jnp.where(y8 == 3, roll(kyhi, 3, 0), own_neighbours[YHI]),
    }
    for blk, kn in neighbours.items():
        alpha[blk] = weigh(k8, kn)


    def ends_of_v1():
        later.extend(send_edges(v1, edge1) + send_y(v1, hy1))

    halo_part(v1, part0, halo_products(gst, hx0, hy0, first), None, ends_of_v1)
    edges1, second = later[:2], later[2:]
    second = second + send_x(v1, hx1)
    parts1 = [send(k_raw, hkc.at[(1 - dx) + (1 - dy) // 2], (dx, dy)) for dx, dy in diagonals]
    own_part(part1, v1, gst, const, None, prod1, True, lambda: parts1.extend(send_y(part1, hpy1)))
    parts1 += send_x(part1, hpx1)

    def coarse_k(k):
        def one(q):
            s = (k[2 * q:2 * q + 1] + k[2 * q + 1:2 * q + 2]) + (k[4 + 2 * q:5 + 2 * q] + k[5 + 2 * q:6 + 2 * q])
            return (s + roll(s, -1)) * 0.125

        return jnp.where(row_even, one(0), roll(one(1), 1))

    kc = coarse_k(k8)
    lane1 = lax.broadcasted_iota(jnp.int32, (1, L), 1)
    cylo, cyhi = coarse_k(kylo), coarse_k(kyhi)
    coarse_neighbours = {
        XLO: coarse_k(kxlo),
        XHI: coarse_k(kxhi),
        YLO: jnp.where(row_even, roll(cylo, -1), roll(kc, 1)),
        YHI: jnp.where(row_even, roll(kc, -1), roll(cyhi, 1)),
        ZLO: jnp.where(lane1 < 2, 0.0, roll(kc, 2)),
        ZHI: jnp.where(lane1 >= L - 2, 0.0, roll(kc, -2)),
    }
    for blk, kn in coarse_neighbours.items():
        calpha[blk:blk + 1, :] = weigh(kc, kn)
    inv_kc = 1.0 / kc

    halo_part(v2, part1, halo_products(gst, hx1, hy1, second, lambda j: parts1.append(
        relay(hy1.at[j, 1 - odd], edge1.at[2 * odd + j], j))), None)

    own_part(part2, v2, rst, rhs, krow, prod, False)
    complete_halo(hx2, hy2, hpx1, hpy1, edge1, edges1 + parts1)
    halo_part(res, part2, halo_products(rst, hx2, hy2), krow)
    r_right = [split_rows(res[x]) for x in range(2)]
    columns = []
    for a in range(2):
        for b in range(2):
            columns.append(jnp.concatenate([r_right[a][:, col(b)], r_right[a][:, col(2 + b)]], axis=1))
    t = dot(qst[...], jnp.concatenate(columns, axis=0))
    packed = jnp.where(even, t[:D, :L] + roll(t[D:, :L], -1), roll(t[:D, L:], 1) + t[D:, L:])
    c1[...] = packed * inv_kc

    third = send_tile(c1, hc1)
    corners2 = [relay(hy2.at[j, 1 - odd], corner2.at[2 * odd + j], j) for j in range(2)]
    for i, product in enumerate(halo_products(gst, hx2, hy2)):
        if i < 2:
            ghx[i] = product
        else:
            ghy[i - 2] = product
    corr1 = c1[...]
    y = dot(gst[D:4 * D, :], split_rows(corr1))
    acc = corr1 + y[:D]
    acc += calpha[ZLO:ZLO + 1, :] * roll(y[D:2 * D], 2)
    acc += calpha[ZHI:ZHI + 1, :] * roll(y[2 * D:], -2)
    arrive(*third)
    acc += calpha[XLO:XLO + 1, :] * dot(gst[block(XLO), :], split_rows(hc1[2]))
    acc += calpha[XHI:XHI + 1, :] * dot(gst[block(XHI), :], split_rows(hc1[3]))
    below = jnp.where(even, roll(hc1[0], -1), roll(corr1, 1))
    acc += calpha[YLO:YLO + 1, :] * dot(gst[block(YLO), :], split_rows(below))
    above = jnp.where(even, roll(corr1, -1), roll(hc1[1], 1))
    acc += calpha[YHI:YHI + 1, :] * dot(gst[block(YHI), :], split_rows(above))
    c2[...] = acc

    fourth = send_tile(c2, hc2)

    def lift(o, q):
        if q == 0:
            return jnp.where(even, o[:D], roll(o[D:], 1))
        return jnp.where(even, roll(o[:D], -1), o[D:])

    def pair(o, i):
        return o[2 * i * D:2 * (i + 1) * D]

    o = dot(pst[...], split_rows(c2[...]))
    for c in range(8):
        x, y = divmod(c, 4)
        q, b = divmod(y, 2)
        lifted[x, :, col(y)] = v2[x, :, col(y)] + lift(pair(o, 2 * x + b), q)
    parts3 = send_edges(lifted, edge3)
    own_part(part3, lifted, gst, const, None, prod1, True, lambda: parts3.extend(send_y(part3, hpy3)))
    parts3 += send_x(part3, hpx3)
    products = []
    passed = []
    arrive(*fourth[:2])
    for j in range(2):
        passed.append(relay(hc2.at[j], corner_c2.at[2 * odd + j], j))
    arrive(*fourth[2:])
    for j in range(2):
        o = dot(gpy[j], split_rows(hc2[j]))
        products.append(ghy[j] + jnp.concatenate([lift(pair(o, x), 1 - j) for x in range(2)], axis=1))
    for i in range(2):
        o = dot(gpx[i], split_rows(hc2[2 + i]))
        products.insert(i, ghx[i] + jnp.concatenate([lift(pair(o, y % 2), y // 2) for y in range(4)], axis=1))
    halo_part(v3, part3, products, None)
    own_part(part0, v3, gst, const, None, prod, False)
    arrive(*corners2, *passed)
    for j in range(2):
        at = 2 * (1 - odd) + j
        rows = pl.ds(pl.multiple_of(odd * 4 * D + (1 - j) * L, L), L)
        edge3[at] = corner2[at] + lift(dot(pst[rows, :], split_rows(corner_c2[at])), 1 - j)
    complete_halo(hx3, hy3, hpx3, hpy3, edge3, parts3)
    halo_part(out, part0, halo_products(gst, hx3, hy3), None)
    for copy, out_if in sent:
        pl.when(out_if)(copy.wait_send)


def on_device(nx, ny, start_field, right_side, coefficient, stiffness, smoother, face_coupling, prolongation):
    flat = lambda x: x.reshape(8 * D, L)
    field = pltpu.VMEM((2, D, 4 * L), F32)
    small = pltpu.VMEM((D, L), F32)
    four = pltpu.VMEM((4, D, L), F32)
    kfour = pltpu.VMEM((4, 8, L), F32)
    xhalo = pltpu.VMEM((2, D, 4 * L), F32)
    yhalo = pltpu.VMEM((2, 2, D, L), F32)
    sends = 42

    def body(*refs):
        kernel(nx, ny, *refs)

    result = pl.pallas_call(
        body,
        out_shape=jax.ShapeDtypeStruct((8 * D, L), F32),
        in_specs=[pl.BlockSpec(memory_space=pltpu.HBM)] * 7,
        out_specs=pl.BlockSpec(memory_space=pltpu.VMEM),
        scratch_shapes=[
            pltpu.VMEM((8 * D, L), F32), pltpu.VMEM((8 * D, L), F32), pltpu.VMEM((8, L), F32),
            pltpu.VMEM((D, D), F32), pltpu.VMEM((D, D), F32), pltpu.VMEM((6, D, D), F32), pltpu.VMEM((8, D, D), F32),
            *[field] * 12, pltpu.VMEM((2, 7 * D, 4 * L), F32), pltpu.VMEM((2, 7 * D, 4 * L), F32),
            *[xhalo, yhalo] * 6, four, four, four, four, kfour, kfour, small, small, four, four,
            pltpu.VMEM((7 * D, 4 * D), BF16), pltpu.VMEM((7 * D, 4 * D), BF16),
            pltpu.VMEM((8 * D, 4 * D), BF16), pltpu.VMEM((2 * D, 16 * D), BF16),
            pltpu.VMEM((2, 4 * D, 4 * D), BF16), pltpu.VMEM((2, 4 * D, 4 * D), BF16), xhalo, pltpu.VMEM((2, D, 2 * L), F32),
            pltpu.VMEM((7, 8, L), F32), pltpu.VMEM((8, L), F32), pltpu.VMEM((2, 8, 4 * L), F32),
            pltpu.SemaphoreType.DMA((7,)), pltpu.SemaphoreType.DMA((sends,)), pltpu.SemaphoreType.DMA((sends,)),
        ],
        compiler_params=pltpu.CompilerParams(
            collective_id=0, has_side_effects=True, vmem_limit_bytes=40 * 2**20),
    )(*(pltpu.with_memory_space_constraint(x, pltpu.HBM) for x in (
        flat(start_field), flat(right_side), coefficient.reshape(8, L), stiffness, smoother, face_coupling,
        prolongation.reshape(8, D, D))))
    return result.reshape(start_field.shape)


def solution(mesh):
    nx, ny = mesh.shape["gx"], mesh.shape["gy"]
    placed = (P(None, "gx", "gy", None), P(None, "gx", "gy", None), P("gx", "gy", None), P(), P(), P(), P())

    def run(*args):
        return on_device(nx, ny, *args)

    return jax.shard_map(
        run, mesh=mesh, in_specs=placed, out_specs=P(None, "gx", "gy", None), check_vma=False)
```

profile of v0, /device:TPU:1, one launch (start us, length us, event | category | flops | bytes accessed | tf_op | source)
XLA Modules:
  0.0 33.9 jit_solution(6663409953249338228)
XLA Ops:
  0.0 33.2 %shard_map.73 = f32[512,128]{1,0:T(8,128)S(1)} custom-call(f32[512,128]{1,0:T(8,128)} %bitcast.6, f32[512,128]{1,0:T(8,128)} %bitcast.7, f32[8,128]{1,0:T(8,128)} %bitcast.9, f32[64,64]{1,0:T(8,128)} %refs_3_.1, f32[64,64]{1,0:T(8,128)} %refs_4_.1, f32[6,64,64]{2,1,0:T(8,128)} %refs_5_.1, f32[8,64,64]{2,1,0:T(8,128)} %bitcast.8), custom_call_target="tpu_custom_call" | custom-call | tf_op jit(solution)/shard_map/pallas_call | solution.py:446
  33.2 0.7 %copy.9 = f32[64,2,4,128]{3,2,1,0:T(4,128)} copy(f32[64,2,4,128]{3,2,1,0:T(4,128)S(1)} %bitcast.5) | data formatting | bytes 524288
where the time goes:
time: 34.1 us; the launch traced here: 33.9 us
  Pallas kernels  33.2 us (97%)
  local copies, waits for them, and re-layouts  0.71 us (2%)
    pallas_call x1, Pallas kernels, on_device(): pl.pallas_call(body, out_shape=jax.ShapeDtypeStruct((8 * D, L), F32), in_...  33.2 us
    unnamed x1, local copies, waits for them, and re-layouts  0.71 us

commit v1 on v0

--- a/solution.py
+++ b/solution.py
@@ -21,11 +21,11 @@
 
 def split_rows(x):
     hi, lo = parts(x)
-    return jnp.concatenate([hi, hi, lo, lo], axis=0)
+    return jnp.concatenate([hi, hi, lo], axis=0)
 
 
 def dot(a, b):
-    return jnp.dot(a, b, preferred_element_type=F32)
+    return jnp.dot(a[:, :b.shape[0]], b, preferred_element_type=F32)
 
 
 def roll(x, shift, axis=1):
@@ -36,11 +36,11 @@
     return slice(c * L, (c + 1) * L)
 
 
-def kernel(nx, ny, v_in, b_in, k_in, s_in, m_in, f_in, p_in, out,
+def kernel(nx, ny, v_in, b_in, k_in, s_in, m_in, f_in, p_in, part0, out_x, out_y, alpha,
            v_raw, b_raw, k_raw, s_raw, m_raw, f_raw, p_raw,
-           v0, v1, v2, v3, rhs, const, res, lifted, part0, part1, part2, part3, prod, prod1,
+           v0, v1, v2, v3, rhs, const, res, lifted, part1, part2, part3, prod, prod1,
            hx0, hy0, hx1, hy1, hpx1, hpy1, hx2, hy2, hpx3, hpy3, hx3, hy3, edge1, edge3, corner2, corner_c2, hk, hkc, c1, c2, hc1, hc2,
-           gst, rst, pst, qst, gpx, gpy, ghx, ghy, alpha, calpha, krow, local_sem, send_sem, recv_sem):
+           gst, rst, pst, qst, gpx, gpy, ghx, ghy, calpha, krow, local_sem, send_sem, recv_sem):
     gx, gy = lax.axis_index("gx"), lax.axis_index("gy")
     has = {(-1, 0): gx > 0, (1, 0): gx < nx - 1, (0, -1): gy > 0, (0, 1): gy < ny - 1}
     for dx in (-1, 1):
@@ -268,10 +268,7 @@
             if scale is not None:
                 acc = acc * scale[x, 0:1, col(y)]
             value = part[x, :, col(y)] + acc
-            if target is out:
-                out[pl.ds(c, D, stride=8), :] = value
-            else:
-                target[x, :, col(y)] = value
+            target[x, :, col(y)] = value
             if c == 7 and ends_done is not None:
                 ends_done()
 
@@ -362,7 +359,7 @@
     for a in range(2):
         for b in range(2):
             columns.append(jnp.concatenate([r_right[a][:, col(b)], r_right[a][:, col(2 + b)]], axis=1))
-    t = dot(qst[...], jnp.concatenate(columns, axis=0))
+    t = sum(dot(qst[:, 4 * D * ab:4 * D * (ab + 1)], columns[ab]) for ab in range(4))
     packed = jnp.where(even, t[:D, :L] + roll(t[D:, :L], -1), roll(t[:D, L:], 1) + t[D:, L:])
     c1[...] = packed * inv_kc
 
@@ -425,9 +422,39 @@
         rows = pl.ds(pl.multiple_of(odd * 4 * D + (1 - j) * L, L), L)
         edge3[at] = corner2[at] + lift(dot(pst[rows, :], split_rows(corner_c2[at])), 1 - j)
     complete_halo(hx3, hy3, hpx3, hpy3, edge3, parts3)
-    halo_part(out, part0, halo_products(gst, hx3, hy3), None)
+    for i, product in enumerate(halo_products(gst, hx3, hy3)):
+        (out_x if i < 2 else out_y)[i % 2] = product
     for copy, out_if in sent:
         pl.when(out_if)(copy.wait_send)
+
+
+def finish_kernel(part, from_x, from_y, alpha, out, buffer, sem):
+    pieces, height = 4, D // 4
+    copies = []
+    for p in range(pieces):
+        rows = slice(p * height, (p + 1) * height)
+        for c in range(8):
+            x, y = divmod(c, 4)
+            value = part[x, rows, col(y)] + alpha[(XLO, XHI)[x], c:c + 1, :] * from_x[x, rows, col(y)]
+            if y in (0, 3):
+                value += alpha[(YLO, YHI)[y // 3], c:c + 1, :] * from_y[y // 3, rows, col(x)]
+            buffer[pl.ds(8 * p * height + c, height, stride=8), :] = value
+        done = slice(8 * p * height, 8 * (p + 1) * height)
+        copies.append(pltpu.make_async_copy(buffer.at[done], out.at[done], sem.at[p]))
+        copies[-1].start()
+    for copy in copies:
+        copy.wait()
+
+
+def finish(*arrays):
+    return pl.pallas_call(
+        finish_kernel,
+        out_shape=jax.ShapeDtypeStruct((8 * D, L), F32),
+        in_specs=[pl.BlockSpec(memory_space=pltpu.VMEM)] * 4,
+        out_specs=pl.BlockSpec(memory_space=pltpu.HBM),
+        scratch_shapes=[pltpu.VMEM((8 * D, L), F32), pltpu.SemaphoreType.DMA((4,))],
+        compiler_params=pltpu.CompilerParams(vmem_limit_bytes=16 * 2**20),
+    )(*arrays)
 
 
 def on_device(nx, ny, start_field, right_side, coefficient, stiffness, smoother, face_coupling, prolongation):
@@ -445,18 +472,19 @@
 
     result = pl.pallas_call(
         body,
-        out_shape=jax.ShapeDtypeStruct((8 * D, L), F32),
+        out_shape=[jax.ShapeDtypeStruct(shape, F32) for shape in (
+            (2, D, 4 * L), (2, D, 4 * L), (2, D, 2 * L), (7, 8, L))],
         in_specs=[pl.BlockSpec(memory_space=pltpu.HBM)] * 7,
-        out_specs=pl.BlockSpec(memory_space=pltpu.VMEM),
+        out_specs=[pl.BlockSpec(memory_space=pltpu.VMEM)] * 4,
         scratch_shapes=[
             pltpu.VMEM((8 * D, L), F32), pltpu.VMEM((8 * D, L), F32), pltpu.VMEM((8, L), F32),
             pltpu.VMEM((D, D), F32), pltpu.VMEM((D, D), F32), pltpu.VMEM((6, D, D), F32), pltpu.VMEM((8, D, D), F32),
-            *[field] * 12, pltpu.VMEM((2, 7 * D, 4 * L), F32), pltpu.VMEM((2, 7 * D, 4 * L), F32),
+            *[field] * 11, pltpu.VMEM((2, 7 * D, 4 * L), F32), pltpu.VMEM((2, 7 * D, 4 * L), F32),
             *[xhalo, yhalo] * 6, four, four, four, four, kfour, kfour, small, small, four, four,
             pltpu.VMEM((7 * D, 4 * D), BF16), pltpu.VMEM((7 * D, 4 * D), BF16),
             pltpu.VMEM((8 * D, 4 * D), BF16), pltpu.VMEM((2 * D, 16 * D), BF16),
             pltpu.VMEM((2, 4 * D, 4 * D), BF16), pltpu.VMEM((2, 4 * D, 4 * D), BF16), xhalo, pltpu.VMEM((2, D, 2 * L), F32),
-            pltpu.VMEM((7, 8, L), F32), pltpu.VMEM((8, L), F32), pltpu.VMEM((2, 8, 4 * L), F32),
+            pltpu.VMEM((8, L), F32), pltpu.VMEM((2, 8, 4 * L), F32),
             pltpu.SemaphoreType.DMA((7,)), pltpu.SemaphoreType.DMA((sends,)), pltpu.SemaphoreType.DMA((sends,)),
         ],
         compiler_params=pltpu.CompilerParams(
@@ -464,7 +492,7 @@
     )(*(pltpu.with_memory_space_constraint(x, pltpu.HBM) for x in (
         flat(start_field), flat(right_side), coefficient.reshape(8, L), stiffness, smoother, face_coupling,
         prolongation.reshape(8, D, D))))
-    return result.reshape(start_field.shape)
+    return finish(*result).reshape(start_field.shape)
 
 
 def solution(mesh):

time: 34.1 us -> 34.1 us (level)
  local copies, waits for them, and re-layouts: 0.71 us -> 0 us
  Pallas kernels: 33.2 us -> 33.9 us
    pallas_call x1 -> x2, Pallas kernels: 33.2 us -> 33.9 us  [the longest x1 33.2 us: on_device(): pl.pallas_call(body, out_shape=[jax.ShapeDtypeStruct(shape, F32) for shap...]
    unnamed x1 -> x0, local copies, waits for them, and re-layouts: 0.71 us -> none
where the time goes in v1:
time: 34.1 us; the launch traced here: 34 us
  Pallas kernels  33.9 us (99%)
    pallas_call x1, Pallas kernels, on_device(): pl.pallas_call(body, out_shape=[jax.ShapeDtypeStruct(shape, F32) for shap...  33.2 us
    pallas_call x1, Pallas kernels, finish(): pl.pallas_call(finish_kernel, out_shape=jax.ShapeDtypeStruct((8 * D, L),...  0.75 us

profile of v1, /device:TPU:1, one launch (start us, length us, event | category | flops | bytes accessed | tf_op | source)
XLA Modules:
  0.0 34.0 jit_solution(10050955209205913599)
XLA Ops:
  0.0 33.2 %shard_map.73 = (f32[2,64,512]{2,1,0:T(8,128)S(1)}, f32[2,64,512]{2,1,0:T(8,128)S(1)}, f32[2,64,256]{2,1,0:T(8,128)S(1)}, f32[7,8,128]{2,1,0:T(8,128)S(1)}) custom-call(f32[512,128]{1,0:T(8,128)} %bitcast.5, f32[512,128]{1,0:T(8,128)} %bitcast.6, f32[8,128]{1,0:T(8,128)} %bitcast.8, f32[64,64]{1,0:T(8,128)} %refs_3_.1, f32[64,64]{1,0:T(8,128)} %refs_4_.1, ...), custom_call_target="tpu_custom_call" | custom-call | tf_op jit(solution)/shard_map/pallas_call | solution.py:473
  33.2 0.7 %shard_map.74 = f32[512,128]{1,0:T(8,128)} custom-call(f32[2,64,512]{2,1,0:T(8,128)S(1)} %get-tuple-element.9.part, f32[2,64,512]{2,1,0:T(8,128)S(1)} %get-tuple-element.10.from_x, f32[2,64,256]{2,1,0:T(8,128)S(1)} %get-tuple-element.11.from_y, f32[7,8,128]{2,1,0:T(8,128)S(1)} %get-tuple-element.12.alpha), custom_call_target="tpu_custom_call" | custom-call | tf_op jit(solution)/shard_map/pallas_call | solution.py:450

commit v2 on v0

--- a/solution.py
+++ b/solution.py
@@ -21,11 +21,11 @@
 
 def split_rows(x):
     hi, lo = parts(x)
-    return jnp.concatenate([hi, hi, lo, lo], axis=0)
+    return jnp.concatenate([hi, hi, lo], axis=0)
 
 
 def dot(a, b):
-    return jnp.dot(a, b, preferred_element_type=F32)
+    return jnp.dot(a[:, :b.shape[0]], b, preferred_element_type=F32)
 
 
 def roll(x, shift, axis=1):
@@ -362,7 +362,7 @@
     for a in range(2):
         for b in range(2):
             columns.append(jnp.concatenate([r_right[a][:, col(b)], r_right[a][:, col(2 + b)]], axis=1))
-    t = dot(qst[...], jnp.concatenate(columns, axis=0))
+    t = sum(dot(qst[:, 4 * D * ab:4 * D * (ab + 1)], columns[ab]) for ab in range(4))
     packed = jnp.where(even, t[:D, :L] + roll(t[D:, :L], -1), roll(t[:D, L:], 1) + t[D:, L:])
     c1[...] = packed * inv_kc
 

time: 34.1 us -> 34.1 us (level)
  no operation moved by 1% of the time
where the time goes in v2:
time: 34.1 us; the launch traced here: 33.9 us
  Pallas kernels  33.2 us (97%)
  local copies, waits for them, and re-layouts  0.71 us (2%)
    pallas_call x1, Pallas kernels, on_device(): pl.pallas_call(body, out_shape=jax.ShapeDtypeStruct((8 * D, L), F32), in_...  33.2 us
    unnamed x1, local copies, waits for them, and re-layouts  0.71 us

profile of v2, /device:TPU:1, one launch (start us, length us, event | category | flops | bytes accessed | tf_op | source)
XLA Modules:
  0.0 33.9 jit_solution(9686720731555514007)
XLA Ops:
  0.0 33.2 %shard_map.73 = f32[512,128]{1,0:T(8,128)S(1)} custom-call(f32[512,128]{1,0:T(8,128)} %bitcast.6, f32[512,128]{1,0:T(8,128)} %bitcast.7, f32[8,128]{1,0:T(8,128)} %bitcast.9, f32[64,64]{1,0:T(8,128)} %refs_3_.1, f32[64,64]{1,0:T(8,128)} %refs_4_.1, f32[6,64,64]{2,1,0:T(8,128)} %refs_5_.1, f32[8,64,64]{2,1,0:T(8,128)} %bitcast.8), custom_call_target="tpu_custom_call" | custom-call | tf_op jit(solution)/shard_map/pallas_call | solution.py:446
  33.2 0.7 %copy.9 = f32[64,2,4,128]{3,2,1,0:T(4,128)} copy(f32[64,2,4,128]{3,2,1,0:T(4,128)S(1)} %bitcast.5) | data formatting | bytes 524288
